TPU v7x, 512 devices: a whole 4x8x8 slice. The times are simulated.
512 devices in a mesh: dp: 64 (over z, x, core), seq: 8 (over y).
Axes of the slice: x: 4, y: 8, z: 8, core: 2. Of those that a mesh axis runs over, the one named last changes fastest.
Arguments:
- queries: bfloat16 [65536, 4096], P(('dp', 'seq')), may hold values from -6 to 6
- keys: bfloat16 [65536, 512], P(('dp', 'seq')), may hold values from -6 to 6
- values: bfloat16 [65536, 512], P(('dp', 'seq')), may hold values from -6 to 6
- grad_out: bfloat16 [65536, 4096], P(('dp', 'seq')), may hold values from -6 to 6
- quant_scale: float32 [2, 4, 128], replicated, may hold values from 2 to 8
- doc_lengths: int32 [64, 8], P('dp'), may hold values from 1 to 512, as said below
Outputs:
- attn_out: bfloat16 [65536, 4096], P(('dp', 'seq'))
- grad_queries: bfloat16 [65536, 4096], P(('dp', 'seq'))
- grad_keys: bfloat16 [65536, 512], P(('dp', 'seq'))
- grad_values: bfloat16 [65536, 512], P(('dp', 'seq'))
- grad_scale: float32 [2, 4, 128], replicated
Inputs may be any that keep to these rules, and one draw needn't show every extreme that they name: `doc_lengths`: each row sums to 1024; its largest length is exactly 512.
All inputs are finite; a program needn't handle non-finite values.
Results may differ from a plain program's by a relative error of at most 0.04.
Values may be sent and summed in bfloat16 or wider, within the bound.
A program may use at most 64 MiB of HBM per device.

v0:
```python
import math

import jax
import jax.numpy as jnp
from jax import lax
from jax.sharding import PartitionSpec as P

two_pi = 2.0 * math.pi


def quantize(source, clip):
    level = 127.0 * jnp.tanh(source / clip)
    return clip / 127.0 * (level - jnp.sin(two_pi * level) / two_pi)


def quant_pair(key_raw, value_raw, clip):
    return (quantize(key_raw, clip[0]), quantize(value_raw, clip[1]))


def segments(lengths, length):
    ends = jnp.cumsum(lengths)
    positions = jnp.arange(length, dtype=jnp.int32)
    return jnp.sum((positions[:, None] >= ends[None, :]).astype(jnp.int32), axis=1)


def attend(query_rows, key_rows, value_rows, grad_rows, segment, row_start, local_kv):
    length = query_rows.shape[0]
    key_len = key_rows.shape[0]
    head_dim = key_rows.shape[1] // local_kv
    per_group = query_rows.shape[1] // (local_kv * head_dim)
    query4 = query_rows.reshape(length, local_kv, per_group, head_dim)
    grad4 = grad_rows.reshape(length, local_kv, per_group, head_dim)
    key3 = key_rows.reshape(key_len, local_kv, head_dim)
    value3 = value_rows.reshape(key_len, local_kv, head_dim)
    block = min(512, length)
    scale = head_dim ** (-0.5)
    columns = jnp.arange(key_len, dtype=jnp.int32)

    def step(carry, index):
        key_acc, value_acc = carry
        start = index * block
        query_blk = lax.dynamic_slice_in_dim(query4, start, block, 0)
        grad_blk = lax.dynamic_slice_in_dim(grad4, start, block, 0)
        row_ids = row_start + start + jnp.arange(block, dtype=jnp.int32)
        row_seg = lax.dynamic_slice_in_dim(segment, row_start + start, block, 0)
        allowed = (columns[None, :] <= row_ids[:, None]) & (segment[None, :] == row_seg[:, None])
        scores = (
            jnp.einsum("qngd,knd->ngqk", query_blk, key3, preferred_element_type=jnp.float32)
            * scale
        )
        scores = jnp.where(allowed, scores, -1e30)
        weights = jnp.exp(scores - jnp.max(scores, axis=-1, keepdims=True))
        probs = weights / jnp.sum(weights, axis=-1, keepdims=True)
        probs_b = probs.astype(jnp.bfloat16)
        output = jnp.einsum(
            "ngqk,knd->qngd", probs_b, value3, preferred_element_type=jnp.float32
        ).astype(jnp.bfloat16)
        delta = jnp.transpose(
            jnp.sum(grad_blk.astype(jnp.float32) * output.astype(jnp.float32), axis=-1), (1, 2, 0)
        )
        dprob = jnp.einsum("qngd,knd->ngqk", grad_blk, value3, preferred_element_type=jnp.float32)
        dscore = (probs * (dprob - delta[..., None]) * scale).astype(jnp.bfloat16)
        grad_query = jnp.einsum(
            "ngqk,knd->qngd", dscore, key3, preferred_element_type=jnp.float32
        ).astype(jnp.bfloat16)
        key_acc = key_acc + jnp.einsum(
            "ngqk,qngd->knd", dscore, query_blk, preferred_element_type=jnp.float32
        )
        value_acc = value_acc + jnp.einsum(
            "ngqk,qngd->knd", probs_b, grad_blk, preferred_element_type=jnp.float32
        )
        return ((key_acc, value_acc), (output, grad_query))

    zeros = jnp.zeros((key_len, local_kv, head_dim), jnp.float32)
    (key_grad, value_grad), (outputs, grad_query) = lax.scan(
        step, (zeros, zeros), jnp.arange(length // block, dtype=jnp.int32)
    )
    return (
        outputs.reshape(length, -1),
        grad_query.reshape(length, -1),
        key_grad.reshape(key_len, -1),
        value_grad.reshape(key_len, -1),
    )


def on_device(queries, keys, values, grad_out, quant_scale, doc_lengths):
    tok_rows = queries.shape[0]
    seq_count = lax.axis_size("seq")
    kv_heads = quant_scale.shape[1]
    head_dim = quant_scale.shape[2]
    slab_rows = tok_rows * seq_count
    segment = segments(doc_lengths[0], slab_rows)
    key_raw = keys.astype(jnp.float32).reshape(tok_rows, kv_heads, head_dim)
    value_raw = values.astype(jnp.float32).reshape(tok_rows, kv_heads, head_dim)
    (key_q, value_q), pull_tokens = jax.vjp(quant_pair, key_raw, value_raw, quant_scale)
    send_key = key_q.astype(jnp.bfloat16).reshape(tok_rows, kv_heads * head_dim)
    send_value = value_q.astype(jnp.bfloat16).reshape(tok_rows, kv_heads * head_dim)
    repeats = max(1, seq_count // kv_heads)
    local_kv = max(1, kv_heads // seq_count)
    query_h, grad_h = (
        lax.all_to_all(queries, "seq", split_axis=1, concat_axis=0, tiled=True),
        lax.all_to_all(grad_out, "seq", split_axis=1, concat_axis=0, tiled=True),
    )

    def widen(array):
        spread = jnp.broadcast_to(
            array.reshape(tok_rows, kv_heads, 1, head_dim), (tok_rows, kv_heads, repeats, head_dim)
        )
        return spread.reshape(tok_rows, kv_heads * repeats * head_dim)

    send_key = widen(send_key)
    send_value = widen(send_value)
    key_h, value_h = (
        lax.all_to_all(send_key, "seq", split_axis=1, concat_axis=0, tiled=True),
        lax.all_to_all(send_value, "seq", split_axis=1, concat_axis=0, tiled=True),
    )
    output_h, grad_query_h, key_grad_h, value_grad_h = attend(
        query_h, key_h, value_h, grad_h, segment, 0, local_kv
    )
    attn_out, grad_queries = (
        lax.all_to_all(output_h, "seq", split_axis=0, concat_axis=1, tiled=True),
        lax.all_to_all(grad_query_h, "seq", split_axis=0, concat_axis=1, tiled=True),
    )
    key_gathered, value_gathered = (
        lax.all_to_all(key_grad_h, "seq", split_axis=0, concat_axis=1, tiled=True),
        lax.all_to_all(value_grad_h, "seq", split_axis=0, concat_axis=1, tiled=True),
    )
    key_sum = jnp.sum(key_gathered.reshape(tok_rows, kv_heads, repeats, head_dim), axis=2)
    value_sum = jnp.sum(value_gathered.reshape(tok_rows, kv_heads, repeats, head_dim), axis=2)
    key_in, value_in, scale_part = pull_tokens((key_sum, value_sum))
    grad_scale = lax.psum(scale_part, ("dp", "seq"))
    grad_keys = key_in.reshape(tok_rows, kv_heads * head_dim).astype(jnp.bfloat16)
    grad_values = value_in.reshape(tok_rows, kv_heads * head_dim).astype(jnp.bfloat16)
    return (attn_out, grad_queries, grad_keys, grad_values, grad_scale)


def solution(mesh):
    return jax.shard_map(
        on_device,
        mesh=mesh,
        in_specs=(
            P(("dp", "seq"), None),
            P(("dp", "seq"), None),
            P(("dp", "seq"), None),
            P(("dp", "seq"), None),
            P(),
            P("dp", None),
        ),
        out_specs=(
            P(("dp", "seq"), None),
            P(("dp", "seq"), None),
            P(("dp", "seq"), None),
            P(("dp", "seq"), None),
            P(),
        ),
        check_vma=False,
    )
```

profile of v0, /device:TPU:1, one launch (start us, length us, event | category | flops | bytes accessed | tf_op | source)
XLA Modules:
  0.0 367.8 jit_solution(9301017761768875349)
XLA Ops:
  4.8 7.7 %all-to-all-start.3 = ((bf16[128,8,128]{0,2,1:T(8,128)(2,1)}), bf16[128,8,128]{0,2,1:T(8,128)(2,1)S(1)}, u32[]{:S(2)}, u32[]{:S(2)}) async-start(bf16[128,8,128]{0,2,1:T(8,128)(2,1)} %bitcast.15), calls=%async_computation.3 | async-start | bytes 524288 | tf_op jit(solution)/shard_map/all_to_all | solution.py:115
  12.5 2.3 copy.101
  14.7 7.1 %all-to-all-done.3 = bf16[128,8,128]{0,2,1:T(8,128)(2,1)S(1)} async-done(((bf16[128,8,128]{0,2,1:T(8,128)(2,1)}), bf16[128,8,128]{0,2,1:T(8,128)(2,1)S(1)}, u32[]{:S(2)}, u32[]{:S(2)}) %all-to-all-start.3) | async-done | bytes 262176 | tf_op jit(solution)/shard_map/all_to_all | solution.py:115
  21.9 3.6 all-to-all-start
  25.4 2.3 copy.105
  27.7 23.7 %all-to-all-done = bf16[128,8,512]{0,2,1:T(8,128)(2,1)S(1)} async-done(((bf16[128,8,512]{0,2,1:T(8,128)(2,1)}), bf16[128,8,512]{0,2,1:T(8,128)(2,1)S(1)}, u32[]{:S(2)}, u32[]{:S(2)}) %all-to-all-start) | async-done | bytes 1048608 | tf_op jit(solution)/shard_map/all_to_all | solution.py:101
  51.4 3.6 all-to-all-start.2
  56.3 24.7 %all-to-all-done.2 = bf16[128,8,512]{0,2,1:T(8,128)(2,1)S(1)} async-done(((bf16[128,8,512]{0,2,1:T(8,128)(2,1)}), bf16[128,8,512]{0,2,1:T(8,128)(2,1)S(1)}, u32[]{:S(2)}, u32[]{:S(2)}) %all-to-all-start.2) | async-done | bytes 1048608 | tf_op jit(solution)/shard_map/all_to_all | solution.py:102
  81.7 3.4 all-to-all-start.1
  90.6 2.3 reshape.296
  94.6 60.3 %while.17 = (s32[]{:T(128)}, f32[1024,1,128]{0,2,1:T(8,128)S(1)}, f32[1024,1,128]{0,2,1:T(8,128)}, bf16[2,512,1,4,128]{4,3,1,0,2:T(4,128)(2,1)}, bf16[2,512,1,4,...) while((s32[]{:T(128)}, f32[1024,1,128]{0,2,1:T(8,128)S(1)}, ...), condition=%wide.region_6.7_spmd.clone, body=%wide.region_2.6_spmd.clone.sunk | while | flops 3277318656 | bytes 84515176 | solution.py:75
  98.3 2.5 fusion.74
  100.7 4.7 %fusion.77 = f32[1024,1,128]{0,2,1:T(8,128)} fusion(f32[1024,1,128]{0,2,1:T(8,128)} %get-tuple-element.341, bf16[1024,1,4,128]{0,3,2,1:T(8,128)(2,1)} %get-tuple-element.363, s32[]{:T(128)S(6)} %select_n.41, pred[]{:T(512)S(6)} %compare.5, f32[4,512]{1,0:T(4,128)S(1)} %fusion.74, f32[4,512]{1,0:T(4,128)S(1)} %get-tuple-element.319, ...), kind=kOutput, calls=%fused_computation.22.clone.1 | convolution fusion | flops 547618816 | bytes 10502149 | tf_op jit(solution)/shard_map/while/body/eval_jaxpr/ngqk,qngd->knd/dot_general | solution.py:69
  105.4 4.3 %multiply_reduce_fusion.4 = (f32[512,4]{0,1:T(4,128)S(1)}, bf16[4,512,128]{1,2,0:T(8,128)(2,1)S(1)}) fusion(bf16[1024,1,4,128]{0,3,2,1:T(8,128)(2,1)} %get-tuple-element.363, s32[]{:T(128)S(6)} %select_n.41, bf16[1024,1,128]{0,2,1:T(8,128)(2,1)S(1)} %get-tuple-element.364, f32[4,512]{1,0:T(4,128)S(1)} %fusion.74, ...), kind=kOutput, calls=%fused_computation.25.clone.1 | convolution fusion | flops 548665344 | bytes 10248196 | tf_op jit(solution)/shard_map/while/body/eval_jaxpr/ngqk,knd->qngd/dot_general | solution.py:55
  109.7 5.9 %fusion.75 = bf16[4,512,1024]{2,1,0:T(8,128)(2,1)} fusion(f32[4,512]{1,0:T(4,128)S(1)} %bitcast.273, f32[4,512]{1,0:T(4,128)S(1)} %fusion.74, f32[4,512]{1,0:T(4,128)S(1)} %get-tuple-element.319, f32[512,4,1024]{2,0,1:T(8,128)S(1)} %get-tuple-element.318, pred[512,1024]{1,0:T(8,128)(4,1)S(1)} %fusion.72, ...), kind=kOutput, calls=%fused_computation.10.clone.1 | convolution fusion | flops 553648128 | bytes 13918212 | tf_op jit(solution)/shard_map/while/body/eval_jaxpr/qngd,knd->ngqk/dot_general | solution.py:61
  116.0 3.2 fusion.76
  119.2 3.4 fusion.78
  128.3 2.5 fusion.74
  130.8 4.9 %fusion.77 = f32[1024,1,128]{0,2,1:T(8,128)} fusion(f32[1024,1,128]{0,2,1:T(8,128)} %get-tuple-element.341, bf16[1024,1,4,128]{0,3,2,1:T(8,128)(2,1)} %get-tuple-element.363, s32[]{:T(128)S(6)} %select_n.41, pred[]{:T(512)S(6)} %compare.5, f32[4,512]{1,0:T(4,128)S(1)} %fusion.74, f32[4,512]{1,0:T(4,128)S(1)} %get-tuple-element.319, ...), kind=kOutput, calls=%fused_computation.22.clone.1 | convolution fusion | flops 547618816 | bytes 10502149 | tf_op jit(solution)/shard_map/while/body/eval_jaxpr/ngqk,qngd->knd/dot_general | solution.py:69
  135.6 4.3 %multiply_reduce_fusion.4 = (f32[512,4]{0,1:T(4,128)S(1)}, bf16[4,512,128]{1,2,0:T(8,128)(2,1)S(1)}) fusion(bf16[1024,1,4,128]{0,3,2,1:T(8,128)(2,1)} %get-tuple-element.363, s32[]{:T(128)S(6)} %select_n.41, bf16[1024,1,128]{0,2,1:T(8,128)(2,1)S(1)} %get-tuple-element.364, f32[4,512]{1,0:T(4,128)S(1)} %fusion.74, ...), kind=kOutput, calls=%fused_computation.25.clone.1 | convolution fusion | flops 548665344 | bytes 10248196 | tf_op jit(solution)/shard_map/while/body/eval_jaxpr/ngqk,knd->qngd/dot_general | solution.py:55
  140.0 5.9 %fusion.75 = bf16[4,512,1024]{2,1,0:T(8,128)(2,1)} fusion(f32[4,512]{1,0:T(4,128)S(1)} %bitcast.273, f32[4,512]{1,0:T(4,128)S(1)} %fusion.74, f32[4,512]{1,0:T(4,128)S(1)} %get-tuple-element.319, f32[512,4,1024]{2,0,1:T(8,128)S(1)} %get-tuple-element.318, pred[512,1024]{1,0:T(8,128)(4,1)S(1)} %fusion.72, ...), kind=kOutput, calls=%fused_computation.10.clone.1 | convolution fusion | flops 553648128 | bytes 13918212 | tf_op jit(solution)/shard_map/while/body/eval_jaxpr/qngd,knd->ngqk/dot_general | solution.py:61
  146.2 3.2 fusion.76
  149.4 3.4 fusion.78
  156.1 5.0 %all-to-all-start.6 = ((f32[8,128,128]{1,2,0:T(8,128)}), f32[8,128,128]{1,2,0:T(8,128)S(1)}, u32[]{:S(2)}, u32[]{:S(2)}) async-start(f32[8,128,128]{1,2,0:T(8,128)} %copy.117), calls=%async_computation.6 | async-start | bytes 1048576 | tf_op jit(solution)/shard_map/all_to_all | solution.py:125
  163.4 10.5 %all-to-all-done.6 = f32[8,128,128]{1,2,0:T(8,128)S(1)} async-done(((f32[8,128,128]{1,2,0:T(8,128)}), f32[8,128,128]{1,2,0:T(8,128)S(1)}, u32[]{:S(2)}, u32[]{:S(2)}) %all-to-all-start.6) | async-done | bytes 524320 | tf_op jit(solution)/shard_map/all_to_all | solution.py:125
  173.8 3.7 %all-to-all-start.7 = ((f32[8,128,128]{1,2,0:T(8,128)}), f32[8,128,128]{1,2,0:T(8,128)S(1)}, u32[]{:S(2)}, u32[]{:S(2)}) async-start(f32[8,128,128]{1,2,0:T(8,128)} %copy.121), calls=%async_computation.7 | async-start | bytes 1048576 | tf_op jit(solution)/shard_map/all_to_all | solution.py:126
  179.8 10.0 %all-to-all-done.7 = f32[8,128,128]{1,2,0:T(8,128)S(1)} async-done(((f32[8,128,128]{1,2,0:T(8,128)}), f32[8,128,128]{1,2,0:T(8,128)S(1)}, u32[]{:S(2)}, u32[]{:S(2)}) %all-to-all-start.7) | async-done | bytes 524320 | tf_op jit(solution)/shard_map/all_to_all | solution.py:126
  189.8 3.6 all-to-all-start.5
  194.6 23.0 %all-to-all-done.5 = bf16[8,128,512]{2,1,0:T(8,128)(2,1)S(1)} async-done(((bf16[8,128,512]{2,1,0:T(8,128)(2,1)}), bf16[8,128,512]{2,1,0:T(8,128)(2,1)S(1)}, u32[]{:S(2)}, u32[]{:S(2)}) %all-to-all-start.5) | async-done | bytes 1048608 | tf_op jit(solution)/shard_map/all_to_all | solution.py:122
  217.6 3.6 all-to-all-start.4
  221.4 2.8 fusion.45
  226.1 137.8 %psum.7 = f32[2,4,128]{2,1,0:T(4,128)} all-reduce(f32[2,4,128]{2,1,0:T(4,128)S(1)} %pad_add_fusion), channel_id=1, replica_groups=mesh['dp'=64,'seq'=8] {'dp','seq'}, use_global_device_ids=true, to_apply=%region_13.14 | all-reduce | flops 1024 | bytes 8192 | tf_op jit(solution)/shard_map/psum | solution.py:131
  (97 shorter events, 36.6 us)
Async XLA Ops:
  0.6 54.4 %copy-start.9 = (bf16[128,512]{1,0:T(8,128)(2,1)S(1)}, bf16[128,512]{1,0:T(8,128)(2,1)}, u32[]{:S(2)}) copy-start(bf16[128,512]{1,0:T(8,128)(2,1)} %param.9) | copy-start | bytes 393220
  0.6 84.6 %copy-start.16 = (s32[1,8]{1,0:T(1,128)S(1)}, s32[1,8]{1,0:T(1,128)}, u32[]{:S(2)}) copy-start(s32[1,8]{1,0:T(1,128)} %param.13) | copy-start | bytes 100
  3.0 82.1 %copy-start = (bf16[128,512]{0,1:T(8,128)(2,1)}, bf16[128,512]{0,1:T(8,128)(2,1)S(1)}, u32[]{:S(2)}) copy-start(bf16[128,512]{0,1:T(8,128)(2,1)S(1)} %copy.107) | copy-start | bytes 393220
  4.8 17.1 %all-to-all-start.3 = ((bf16[128,8,128]{0,2,1:T(8,128)(2,1)}), bf16[128,8,128]{0,2,1:T(8,128)(2,1)S(1)}, u32[]{:S(2)}, u32[]{:S(2)}) async-start(bf16[128,8,128]{0,2,1:T(8,128)(2,1)} %bitcast.15), calls=%async_computation.3 | async-start | bytes 524288 | tf_op jit(solution)/shard_map/all_to_all | solution.py:115
  21.9 29.6 %all-to-all-start = ((bf16[128,8,512]{0,2,1:T(8,128)(2,1)}), bf16[128,8,512]{0,2,1:T(8,128)(2,1)S(1)}, u32[]{:S(2)}, u32[]{:S(2)}) async-start(bf16[128,8,512]{0,2,1:T(8,128)(2,1)} %bitcast), calls=%async_computation | async-start | bytes 2097152 | tf_op jit(solution)/shard_map/all_to_all | solution.py:101
  51.4 29.6 %all-to-all-start.2 = ((bf16[128,8,512]{0,2,1:T(8,128)(2,1)}), bf16[128,8,512]{0,2,1:T(8,128)(2,1)S(1)}, u32[]{:S(2)}, u32[]{:S(2)}) async-start(bf16[128,8,512]{0,2,1:T(8,128)(2,1)} %bitcast.263), calls=%async_computation.2 | async-start | bytes 2097152 | tf_op jit(solution)/shard_map/all_to_all | solution.py:102
  55.1 30.0 %copy-start.2 = (bf16[128,512]{0,1:T(8,128)(2,1)}, bf16[128,512]{0,1:T(8,128)(2,1)S(1)}, u32[]{:S(2)}) copy-start(bf16[128,512]{0,1:T(8,128)(2,1)S(1)} %copy.103) | copy-start | bytes 393220
  81.7 12.8 %all-to-all-start.1 = ((bf16[128,8,128]{2,0,1:T(8,128)(2,1)}), bf16[128,8,128]{2,0,1:T(8,128)(2,1)S(1)}, u32[]{:S(2)}, u32[]{:S(2)}) async-start(bf16[128,8,128]{2,0,1:T(8,128)(2,1)} %bitcast.7), calls=%async_computation.1 | async-start | bytes 524288 | tf_op jit(solution)/shard_map/all_to_all | solution.py:114
  116.0 6.6 %copy-start.4 = (bf16[2,512,1,4,128]{4,3,1,0,2:T(4,128)(2,1)S(1)}, bf16[2,512,1,4,128]{4,3,1,0,2:T(4,128)(2,1)}, u32[]{:S(2)}) copy-start(bf16[2,512,1,4,128]{4,3,1,0,2:T(4,128)(2,1)} %get-tuple-element.343) | copy-start | bytes 3145732 | tf_op jit(solution)/shard_map/while
  116.0 6.6 %copy-start.6 = (bf16[2,512,1,4,128]{4,3,1,0,2:T(4,128)(2,1)S(1)}, bf16[2,512,1,4,128]{4,3,1,0,2:T(4,128)(2,1)}, u32[]{:S(2)}) copy-start(bf16[2,512,1,4,128]{4,3,1,0,2:T(4,128)(2,1)} %get-tuple-element.342) | copy-start | bytes 3145732 | tf_op jit(solution)/shard_map/while
  123.3 1.0 copy-start.5
  123.3 1.3 copy-start.7
  146.2 6.6 %copy-start.4 = (bf16[2,512,1,4,128]{4,3,1,0,2:T(4,128)(2,1)S(1)}, bf16[2,512,1,4,128]{4,3,1,0,2:T(4,128)(2,1)}, u32[]{:S(2)}) copy-start(bf16[2,512,1,4,128]{4,3,1,0,2:T(4,128)(2,1)} %get-tuple-element.343) | copy-start | bytes 3145732 | tf_op jit(solution)/shard_map/while
  146.2 6.6 %copy-start.6 = (bf16[2,512,1,4,128]{4,3,1,0,2:T(4,128)(2,1)S(1)}, bf16[2,512,1,4,128]{4,3,1,0,2:T(4,128)(2,1)}, u32[]{:S(2)}) copy-start(bf16[2,512,1,4,128]{4,3,1,0,2:T(4,128)(2,1)} %get-tuple-element.342) | copy-start | bytes 3145732 | tf_op jit(solution)/shard_map/while
  153.5 1.0 copy-start.5
  153.5 1.3 copy-start.7
  154.8 38.5 %copy-start.8 = (bf16[2,512,1,4,128]{4,3,1,0,2:T(4,128)(2,1)S(1)}, bf16[2,512,1,4,128]{4,3,1,0,2:T(4,128)(2,1)}, u32[]{:S(2)}) copy-start(bf16[2,512,1,4,128]{4,3,1,0,2:T(4,128)(2,1)} %get-tuple-element.70) | copy-start | bytes 3145732
  154.8 66.4 %copy-start.1 = (bf16[128,512]{0,1:T(8,128)(2,1)S(1)}, bf16[128,512]{0,1:T(8,128)(2,1)}, u32[]{:S(2)}) copy-start(bf16[128,512]{0,1:T(8,128)(2,1)} %copy-done) | copy-start | bytes 393220
  154.8 66.5 %copy-start.3 = (bf16[128,512]{0,1:T(8,128)(2,1)S(1)}, bf16[128,512]{0,1:T(8,128)(2,1)}, u32[]{:S(2)}) copy-start(bf16[128,512]{0,1:T(8,128)(2,1)} %copy-done.2) | copy-start | bytes 393220
  154.8 66.5 %copy-start.10 = (f32[512]{0:T(512)S(1)}, f32[512]{0:T(512)}, u32[]{:S(2)}) copy-start(f32[512]{0:T(512)} %get-tuple-element.234) | copy-start | bytes 6148
  154.8 66.5 %copy-start.11 = (f32[512]{0:T(512)S(1)}, f32[512]{0:T(512)}, u32[]{:S(2)}) copy-start(f32[512]{0:T(512)} %get-tuple-element.238) | copy-start | bytes 6148
  154.9 66.5 %copy-start.12 = (f32[512]{0:T(512)S(1)}, f32[512]{0:T(512)}, u32[]{:S(2)}) copy-start(f32[512]{0:T(512)} %get-tuple-element.232) | copy-start | bytes 6148
  154.9 66.5 %copy-start.13 = (f32[512]{0:T(512)S(1)}, f32[512]{0:T(512)}, u32[]{:S(2)}) copy-start(f32[512]{0:T(512)} %get-tuple-element.235) | copy-start | bytes 6148
  154.9 66.5 %copy-start.14 = (f32[512]{0:T(512)S(1)}, f32[512]{0:T(512)}, u32[]{:S(2)}) copy-start(f32[512]{0:T(512)} %get-tuple-element.236) | copy-start | bytes 6148
  154.9 66.5 %copy-start.15 = (f32[512]{0:T(512)S(1)}, f32[512]{0:T(512)}, u32[]{:S(2)}) copy-start(f32[512]{0:T(512)} %get-tuple-element.239) | copy-start | bytes 6148
  156.1 17.8 %all-to-all-start.6 = ((f32[8,128,128]{1,2,0:T(8,128)}), f32[8,128,128]{1,2,0:T(8,128)S(1)}, u32[]{:S(2)}, u32[]{:S(2)}) async-start(f32[8,128,128]{1,2,0:T(8,128)} %copy.117), calls=%async_computation.6 | async-start | bytes 1048576 | tf_op jit(solution)/shard_map/all_to_all | solution.py:125
  173.8 16.0 %all-to-all-start.7 = ((f32[8,128,128]{1,2,0:T(8,128)}), f32[8,128,128]{1,2,0:T(8,128)S(1)}, u32[]{:S(2)}, u32[]{:S(2)}) async-start(f32[8,128,128]{1,2,0:T(8,128)} %copy.121), calls=%async_computation.7 | async-start | bytes 1048576 | tf_op jit(solution)/shard_map/all_to_all | solution.py:126
  189.8 27.8 %all-to-all-start.5 = ((bf16[8,128,512]{2,1,0:T(8,128)(2,1)}), bf16[8,128,512]{2,1,0:T(8,128)(2,1)S(1)}, u32[]{:S(2)}, u32[]{:S(2)}) async-start(bf16[8,128,512]{2,1,0:T(8,128)(2,1)} %all_to_all.116), calls=%async_computation.5 | async-start | bytes 2097152 | tf_op jit(solution)/shard_map/all_to_all | solution.py:122
  217.6 148.2 %all-to-all-start.4 = ((bf16[8,128,512]{2,1,0:T(8,128)(2,1)}), bf16[8,128,512]{2,1,0:T(8,128)(2,1)S(1)}, u32[]{:S(2)}, u32[]{:S(2)}) async-start(bf16[8,128,512]{2,1,0:T(8,128)(2,1)} %all_to_all.112), calls=%async_computation.4 | async-start | bytes 2097152 | tf_op jit(solution)/shard_map/all_to_all | solution.py:121
where the time goes:
time: 370 us; the launch traced here: 368 us
  blocking collectives  138 us (37%)
  waiting for transfers between devices  101 us (27%)
  matrix products  46.9 us (13%)
  starting transfers between devices  34 us (9%)
  local copies, waits for them, and re-layouts  33.1 us (9%)
  other arithmetic  12.8 us (3%)
    psum x1, blocking collectives, on_device(): grad_scale = lax.psum(scale_part, ('dp', 'seq'))  138 us
    all_to_all x1, waiting for transfers between devices, on_device(): lax.all_to_all(grad_out, 'seq', split_axis=1, concat_axis=0, tiled=True)  24.7 us
    all_to_all x1, waiting for transfers between devices, on_device(): lax.all_to_all(queries, 'seq', split_axis=1, concat_axis=0, tiled=True)  23.7 us
    all_to_all x1, waiting for transfers between devices, on_device(): lax.all_to_all(grad_query_h, 'seq', split_axis=0, concat_axis=1, tiled=True)  23 us
    dot_general x2, matrix products, step(): jnp.einsum('qngd,knd->ngqk', grad_blk, value3, preferred_element_type=jnp...  11.8 us
    all_to_all x1, waiting for transfers between devices, on_device(): lax.all_to_all(key_grad_h, 'seq', split_axis=0, concat_axis=1, tiled=True)  10.5 us
    unnamed x35, local copies, waits for them, and re-layouts  10 us
    all_to_all x1, waiting for transfers between devices, on_device(): lax.all_to_all(value_grad_h, 'seq', split_axis=0, concat_axis=1, tiled=True)  10 us
  transfers between devices with their start and end apart: 8, of which 7 were waited for; matrix products, arithmetic and copies ran while one was open for 6% of the time, Pallas kernels for 0%

commit v1 on v0

v1 whole, which is shorter than its diff:
```python
import functools
import math

import jax
import jax.numpy as jnp
from jax import lax
from jax.experimental import pallas as pl
from jax.experimental.pallas import tpu as pltpu
from jax.sharding import PartitionSpec as P

MESH = pl.DeviceIdType.MESH
HD = 128
BACK = 4
WIN = (BACK + 1) * HD
GROUP = 2
SCALE = HD**-0.5


def transposed_lhs(a, b):
    return lax.dot_general(a, b, (((0,), (0,)), ((), ())), preferred_element_type=jnp.float32)


def dot_nt(a, b):
    return lax.dot_general(a, b, (((1,), (1,)), ((), ())), preferred_element_type=jnp.float32)


def dot(a, b):
    return jnp.dot(a, b, preferred_element_type=jnp.float32)


def quantize(x, c):
    ratio = x / c
    t = jnp.tanh(ratio)
    u = 127.0 * t
    angle = math.pi * (u - jnp.floor(u + 0.5))
    s = jnp.sin(angle)
    level = u - s * jnp.cos(angle) * (1.0 / math.pi)
    by_x = (1.0 - t * t) * (2.0 * s * s)
    return (c * (1.0 / 127.0)) * level, by_x, level * (1.0 / 127.0) - ratio * by_x


def attend_step(q, g, keys, values, bias):
    rows = q.shape[0]
    s = dot_nt(q, keys) * (SCALE * math.log2(math.e))
    s = (s.reshape(rows // HD, HD, WIN) + bias[None]).reshape(rows, WIN)
    p = jnp.exp2(s - jnp.max(s, axis=1, keepdims=True))
    inv = 1.0 / jnp.sum(p, axis=1, keepdims=True)
    p_b = p.astype(jnp.bfloat16)
    out = dot(p_b, values) * inv
    g_n = (g.astype(jnp.float32) * inv).astype(jnp.bfloat16)
    delta = jnp.sum(g_n.astype(jnp.float32) * out, axis=1, keepdims=True)
    ds = (p * (dot_nt(g_n, values) - delta)).astype(jnp.bfloat16)
    dq = dot(ds, keys) * SCALE
    return out, dq, transposed_lhs(q, ds), transposed_lhs(g_n, p_b)


def kernel(
    kvh, q_hbm, g_hbm, k_ref, v_ref, clip_ref, doc_ref,
    o_hbm, dq_hbm, gk_ref, gv_ref, gs_ref,
    q_buf, g_buf, o_buf, dq_buf, kv, part, sbuf, rbuf, bias, dx, dc, ar_src, ar_buf,
    in_sem, out_sem, fs, fr, bs, br, ars, arr,
):
    n_seq, n_dp = lax.axis_size("seq"), lax.axis_size("dp")
    me, dp = lax.axis_index("seq"), lax.axis_index("dp")
    n_w = min(8, n_dp)
    n_z = n_dp // n_w
    w, z = lax.rem(dp, n_w), dp // n_w
    nxt, prv = lax.rem(me + 1, n_seq), lax.rem(me + n_seq - 1, n_seq)
    per_kv = q_hbm.shape[1] // kvh

    def columns(h):
        return pl.ds(pl.multiple_of(h * per_kv, HD), per_kv)

    def loads(h):
        return (
            pltpu.make_async_copy(q_hbm.at[:, columns(h)], q_buf.at[h], in_sem.at[h, 0]),
            pltpu.make_async_copy(g_hbm.at[:, columns(h)], g_buf.at[h], in_sem.at[h, 1]),
        )

    def stores(h):
        return (
            pltpu.make_async_copy(o_buf.at[h], o_hbm.at[:, columns(h)], out_sem.at[h, 0]),
            pltpu.make_async_copy(dq_buf.at[h], dq_hbm.at[:, columns(h)], out_sem.at[h, 1]),
        )

    for h in range(kvh):
        for copy in loads(h):
            copy.start()

    phases = []
    for mine, count, where in (
        (me, n_seq, lambda i: {"seq": i}),
        (w, n_w, lambda i: {"dp": z * n_w + i}),
        (z, n_z, lambda i: {"dp": i * n_w + w}),
    ):
        if count > 1:
            phases.append((len(phases), mine, count, where))

    barrier = pltpu.get_barrier_semaphore()
    greeted = 0
    for _, mine, count, where in phases:
        for off in range(1, count):
            pl.semaphore_signal(
                barrier, inc=1, device_id=where(lax.rem(mine + off, count)), device_id_type=MESH
            )
            greeted += 1

    def quantize_head(h):
        for t, ref in enumerate((k_ref, v_ref)):
            x = ref[:, h * HD : (h + 1) * HD].astype(jnp.float32)
            value, by_x, by_c = quantize(x, clip_ref[t * kvh + h : t * kvh + h + 1, :])
            kv[h, t, 0:HD, :] = value.astype(jnp.bfloat16)
            dx[h, t] = by_x
            dc[h, t] = by_c

    def fwd(h, d):
        return pltpu.make_async_remote_copy(
            src_ref=kv.at[h, :, pl.ds(d * HD, HD), :],
            dst_ref=kv.at[h, :, pl.ds((d + 1) * HD, HD), :],
            send_sem=fs.at[h, d],
            recv_sem=fr.at[h, d],
            device_id={"seq": nxt},
            device_id_type=MESH,
        )

    def bwd(h, t):
        return pltpu.make_async_remote_copy(
            src_ref=sbuf.at[h, t - 1],
            dst_ref=rbuf.at[h, t - 1],
            send_sem=bs.at[h, t - 1],
            recv_sem=br.at[h, t - 1],
            device_id={"seq": prv},
            device_id_type=MESH,
        )

    def relay(h, d):
        fwd(h, d - 1).wait_recv()
        fwd(h, d).start()

    def give_back(h, t):
        total = part[h, :, :, t * HD : (t + 1) * HD]
        if t < BACK:
            bwd(h, t + 1).wait_recv()
            total = total + rbuf[h, t].astype(jnp.float32)
        sbuf[h, t - 1] = total.astype(jnp.bfloat16)
        bwd(h, t).start()

    def finish(h):
        bwd(h, 1).wait_recv()
        here = pl.ds(pl.multiple_of(h * HD, HD), HD)
        for t, ref in enumerate((gk_ref, gv_ref)):
            total = part[h, t, :, 0:HD] + rbuf[h, 0, t].astype(jnp.float32)
            total = total.T
            if t == 0:
                total = total * SCALE
            ref[:, here] = (total * dx[h, t]).astype(ref.dtype)
            ar_src[0, pl.ds(t * kvh + h, 1), :] = jnp.sum(total * dc[h, t], axis=0, keepdims=True)

    quantize_head(0)
    pl.semaphore_wait(barrier, greeted)
    fwd(0, 0).start()
    quantize_head(1)
    fwd(1, 0).start()
    quantize_head(2)
    relay(0, 1)
    fwd(2, 0).start()
    quantize_head(3)

    row = lax.broadcasted_iota(jnp.int32, (HD, WIN), 0) + me * HD
    col = lax.broadcasted_iota(jnp.int32, (HD, WIN), 1)
    key = me * HD + lax.rem(col, HD) - (col // HD) * HD
    end = jnp.int32(0)
    first = jnp.zeros((HD, WIN), jnp.int32)
    for i in range(doc_ref.shape[1]):
        end = end + doc_ref[0, i]
        first = jnp.where(row >= end, end, first)
    bias[...] = jnp.where((key >= first) & (key <= row), 0.0, -1e30)

    relay(0, 2)
    relay(1, 1)
    relay(0, 3)

    steps = per_kv // (GROUP * HD)

    def one_head(h, _):
        def after(step):
            if step == 0:

                @pl.when(h + 3 < kvh)
                def _():
                    fwd(h + 3, 0).start()

                @pl.when(h + 1 < kvh)
                def _():
                    relay(h + 1, 2)

                @pl.when(h >= 1)
                def _():
                    give_back(h - 1, 3)

            if step == steps // 4:

                @pl.when(h + 2 < kvh)
                def _():
                    relay(h + 2, 1)

                @pl.when(h >= 1)
                def _():
                    give_back(h - 1, 2)

            if step == steps // 2:

                @pl.when(h + 1 < kvh)
                def _():
                    relay(h + 1, 3)

                @pl.when(h >= 1)
                def _():
                    give_back(h - 1, 1)

            if step == steps - 1:
                give_back(h, 4)

                @pl.when(h >= 2)
                def _():
                    finish(h - 2)

        for copy in loads(h):
            copy.wait()
        fwd(h, 3).wait_recv()
        for step in range(steps):
            lanes = [
                slice((step * GROUP + i) * HD, (step * GROUP + i + 1) * HD) for i in range(GROUP)
            ]
            q = jnp.concatenate([q_buf[h, :, at] for at in lanes], axis=0)
            g = jnp.concatenate([g_buf[h, :, at] for at in lanes], axis=0)
            out, dq, dk_t, dv_t = attend_step(q, g, kv[h, 0], kv[h, 1], bias[...])
            for i, at in enumerate(lanes):
                o_buf[h, :, at] = out[i * HD : (i + 1) * HD].astype(jnp.bfloat16)
                dq_buf[h, :, at] = dq[i * HD : (i + 1) * HD].astype(jnp.bfloat16)
            if step == 0:
                part[h, 0] = dk_t
                part[h, 1] = dv_t
            else:
                part[h, 0] += dk_t
                part[h, 1] += dv_t
            if step == steps - 1:
                for copy in stores(h):
                    copy.start()
            after(step)
        return 0

    lax.fori_loop(0, kvh, one_head, 0)

    last = kvh - 1
    give_back(last, 3)
    finish(last - 1)
    give_back(last, 2)
    give_back(last, 1)
    finish(last)

    def exchange(phase, mine, count, where, off, slot):
        return pltpu.make_async_remote_copy(
            src_ref=ar_src.at[phase],
            dst_ref=ar_buf.at[phase, slot],
            send_sem=ars.at[phase, off],
            recv_sem=arr.at[phase, off],
            device_id=where(lax.rem(mine + off, count)),
            device_id_type=MESH,
        )

    for phase, mine, count, where in phases:
        for off in range(1, count):
            exchange(phase, mine, count, where, off, mine).start()
        ar_buf[phase, mine] = ar_src[phase]
        for off in range(1, count):
            source = lax.rem(mine + count - off, count)
            exchange(phase, mine, count, where, off, source).wait_recv()
        total = ar_buf[phase, 0]
        for i in range(1, count):
            total = total + ar_buf[phase, i]
        ar_src[phase + 1] = total
    gs_ref[...] = ar_src[len(phases)]

    for phase, mine, count, where in phases:
        for off in range(1, count):
            exchange(phase, mine, count, where, off, mine).wait_send()
    for h in range(kvh):
        for d in range(BACK):
            fwd(h, d).wait_send()
            bwd(h, d + 1).wait_send()
        for copy in stores(h):
            copy.wait()


def on_device(queries, keys, values, grad_out, quant_scale, doc_lengths):
    rows, width = queries.shape
    kvh = quant_scale.shape[1]
    per_kv = width // kvh
    bf16, f32 = jnp.bfloat16, jnp.float32
    dma = pltpu.SemaphoreType.DMA
    vmem = pl.BlockSpec(memory_space=pltpu.VMEM)
    hbm = pl.BlockSpec(memory_space=pl.ANY)
    out, dq, gk, gv, gs = pl.pallas_call(
        functools.partial(kernel, kvh),
        out_shape=(
            jax.ShapeDtypeStruct(queries.shape, bf16),
            jax.ShapeDtypeStruct(queries.shape, bf16),
            jax.ShapeDtypeStruct(keys.shape, bf16),
            jax.ShapeDtypeStruct(values.shape, bf16),
            jax.ShapeDtypeStruct((2 * kvh, HD), f32),
        ),
        in_specs=[hbm, hbm, vmem, vmem, vmem, pl.BlockSpec(memory_space=pltpu.SMEM)],
        out_specs=(hbm, hbm, vmem, vmem, vmem),
        scratch_shapes=[
            pltpu.VMEM((kvh, rows, per_kv), bf16),
            pltpu.VMEM((kvh, rows, per_kv), bf16),
            pltpu.VMEM((kvh, rows, per_kv), bf16),
            pltpu.VMEM((kvh, rows, per_kv), bf16),
            pltpu.VMEM((kvh, 2, WIN, HD), bf16),
            pltpu.VMEM((kvh, 2, HD, WIN), f32),
            pltpu.VMEM((kvh, BACK, 2, HD, HD), bf16),
            pltpu.VMEM((kvh, BACK, 2, HD, HD), bf16),
            pltpu.VMEM((HD, WIN), f32),
            pltpu.VMEM((kvh, 2, rows, HD), f32),
            pltpu.VMEM((kvh, 2, rows, HD), f32),
            pltpu.VMEM((4, 2 * kvh, HD), f32),
            pltpu.VMEM((3, 8, 2 * kvh, HD), f32),
            dma((kvh, 2)),
            dma((kvh, 2)),
            dma((kvh, BACK)),
            dma((kvh, BACK)),
            dma((kvh, BACK)),
            dma((kvh, BACK)),
            dma((3, 8)),
            dma((3, 8)),
        ],
        compiler_params=pltpu.CompilerParams(
            collective_id=0, has_side_effects=True, vmem_limit_bytes=48 * 2**20
        ),
    )(queries, grad_out, keys, values, quant_scale.reshape(2 * kvh, HD), doc_lengths)
    return (out, dq, gk, gv, gs.reshape(quant_scale.shape))


def solution(mesh):
    rows = P(("dp", "seq"), None)
    return jax.shard_map(
        on_device,
        mesh=mesh,
        in_specs=(rows, rows, rows, rows, P(), P("dp", None)),
        out_specs=(rows, rows, rows, rows, P()),
        check_vma=False,
    )
```

time: 370 us -> 112 us (0.30)
  blocking collectives: 138 us -> 0 us
  Pallas kernels: 0 us -> 101 us
  waiting for transfers between devices: 101 us -> 0 us
  matrix products: 46.9 us -> 0 us
  starting transfers between devices: 34 us -> 0 us
  local copies, waits for them, and re-layouts: 33.1 us -> 9.43 us
  other arithmetic: 12.8 us -> 0 us
    psum x1 -> x0, blocking collectives: 138 us -> none  [on_device(): grad_scale = lax.psum(scale_part, ('dp', 'seq'))]
    pallas_call x0 -> x1, Pallas kernels: none -> 101 us  [on_device(): pl.pallas_call(functools.partial(kernel, kvh), out_shape=(jax.ShapeDtypeS...]
    all_to_all x8 -> x0, waiting for transfers between devices: 101 us -> none  [the longest x1 24.7 us: on_device(): lax.all_to_all(grad_out, 'seq', split_axis=1, concat_axis=0, tiled=True)]
    dot_general x12 -> x0, matrix products: 46.9 us -> none  [the longest x2 11.8 us: step(): jnp.einsum('qngd,knd->ngqk', grad_blk, value3, preferred_element_type=jnp...]
    all_to_all x8 -> x0, starting transfers between devices: 34 us -> none  [the longest x1 7.65 us: on_device(): lax.all_to_all(send_value, 'seq', split_axis=1, concat_axis=0, tiled=True)]
    all_to_all x9 -> x0, local copies, waits for them, and re-layouts: 10.2 us -> none  [the longest x2 2.89 us: on_device(): lax.all_to_all(grad_query_h, 'seq', split_axis=0, concat_axis=1, tiled=True)]
    reduce_sum x6 -> x0, other arithmetic: 7.92 us -> none  [the longest x2 4.93 us: step(): probs = weights / jnp.sum(weights, axis=-1, keepdims=True)]
    while x18 -> x0, local copies, waits for them, and re-layouts: 4.05 us -> none
  transfers between devices with their start and end apart: 8 -> 0, of which waited for: 7 -> 0; matrix products, arithmetic and copies ran while one was open for 6% -> 0% of each run, Pallas kernels for 0% -> 0%
where the time goes in v1:
time: 112 us; the launch traced here: 111 us
  Pallas kernels  101 us (90%)
  local copies, waits for them, and re-layouts  9.43 us (8%)
    pallas_call x1, Pallas kernels, on_device(): pl.pallas_call(functools.partial(kernel, kvh), out_shape=(jax.ShapeDtypeS...  101 us
    unnamed x17, local copies, waits for them, and re-layouts  9.43 us

profile of v1, /device:TPU:1, one launch (start us, length us, event | category | flops | bytes accessed | tf_op | source)
XLA Modules:
  0.0 111.4 jit_solution(7759958561439225450)
XLA Ops:
  0.6 0.0 copy-start.5
  0.6 0.6 copy-done.5
  1.3 0.0 copy-start
  1.3 1.2 %copy-done = bf16[128,4096]{1,0:T(8,128)(2,1)S(1)} copy-done((bf16[128,4096]{1,0:T(8,128)(2,1)S(1)}, bf16[128,4096]{1,0:T(8,128)(2,1)}, u32[]{:S(2)}) %copy-start) | copy-done | bytes 1048600
  2.5 0.0 copy-start.1
  2.5 1.2 %copy-done.1 = bf16[128,4096]{1,0:T(8,128)(2,1)S(1)} copy-done((bf16[128,4096]{1,0:T(8,128)(2,1)S(1)}, bf16[128,4096]{1,0:T(8,128)(2,1)}, u32[]{:S(2)}) %copy-start.1) | copy-done | bytes 1048600
  3.7 0.0 copy-start.2
  3.7 0.9 copy-done.2
  4.6 0.0 copy-start.3
  4.6 0.9 copy-done.3
  5.5 0.0 copy-start.4
  5.6 0.7 copy-done.4
  6.2 101.3 %shard_map.101 = (bf16[128,4096]{1,0:T(8,128)(2,1)S(1)}, bf16[128,4096]{1,0:T(8,128)(2,1)S(1)}, bf16[128,512]{1,0:T(8,128)(2,1)S(1)}, bf16[128,512]{1,0:T(8,128)(2,1)S(1)}, f32[8,128]{1,0:T(8,128)S(1)}) custom-call(bf16[128,4096]{1,0:T(8,128)(2,1)S(1)} %copy-done, bf16[128,4096]{1,0:T(8,128)(2,1)S(1)} %copy-done.1, bf16[128,512]{1,0:T(8,128)(2,1)S(1)} %copy-done.2, ...), custom_call_target="tpu_custom_call" | custom-call | tf_op jit(solution)/shard_map/pallas_call | solution.py:304
  107.6 1.0 copy.16
  108.5 1.0 copy.17
  109.5 0.7 copy.18
  110.2 0.7 copy.19
  110.8 0.6 copy.20
Async XLA Ops:
  0.6 0.7 copy-start.5
  1.3 1.2 %copy-start = (bf16[128,4096]{1,0:T(8,128)(2,1)S(1)}, bf16[128,4096]{1,0:T(8,128)(2,1)}, u32[]{:S(2)}) copy-start(bf16[128,4096]{1,0:T(8,128)(2,1)} %q_hbm.1) | copy-start | bytes 3145732
  2.5 1.2 %copy-start.1 = (bf16[128,4096]{1,0:T(8,128)(2,1)S(1)}, bf16[128,4096]{1,0:T(8,128)(2,1)}, u32[]{:S(2)}) copy-start(bf16[128,4096]{1,0:T(8,128)(2,1)} %g_hbm.1) | copy-start | bytes 3145732
  3.7 0.9 copy-start.2
  4.6 0.9 copy-start.3
  5.5 0.7 copy-start.4
